TPU v7x, 256 devices: a whole 4x4x8 slice. The times are simulated.
256 devices in a mesh: row: 32 (over z_hi, y, core), col: 8 (over x, z_lo).
Axes of the slice: x: 4, y: 4, z: 8 (z_hi: 4, z_lo: 2; z = z_hi * 2 + z_lo), core: 2. Of those that a mesh axis runs over, the one named last changes fastest.
Arguments:
- blocks: bfloat16 [32, 8, 16, 128, 128], P('row', 'col'), may hold values from -1.5 to 1.5
- slot_rows: int32 [32, 8, 16], P('row', 'col'), may hold values from 0 to 19, as said below
- slot_cols: int32 [32, 8, 16], P('row', 'col'), may hold values from 0 to 1
- counts: int32 [32, 8], P('row', 'col'), may hold values from 8 to 16, as said below
- col_window: int32 [8, 2], P('col'), may hold values from 0 to 79
Outputs:
- panel_product: float32 [640, 16, 128, 128], P('row', 'col')
Inputs may be any that keep to these rules, and one draw needn't show every extreme that they name: `slot_rows`: within one device, the live slots name distinct positions. `counts`: 16 is reached on some device.
All inputs are finite; a program needn't handle non-finite values.
Results may differ from a plain program's by a relative error of at most 0.0003.
Values may be sent and summed in bfloat16 or wider, within the bound.
A program may use at most 128 MiB of HBM per device.

v0:
```python
import jax
import jax.numpy as jnp
from jax import lax
from jax.sharding import PartitionSpec as P

KP = 16
RL = 20


def broadcast(value, axis, source):
    kept = jnp.where(lax.axis_index(axis) == source, value, 0).astype(value.dtype)
    return lax.psum(kept, axis)


def build_strips(stored, row_slots, col_slots, live_counts, targets, enabled):
    sources = stored.shape[0]
    slot_count = stored.shape[1]
    width = stored.shape[2]
    per_source = KP // sources
    live_slots = jnp.arange(slot_count)[None, :] < live_counts[:, None]
    column_ids = jnp.arange(per_source)
    matches = row_slots[None, :, None, :] == targets[:, None, None, None]
    matches = matches & (col_slots[None, :, None, :] == column_ids[None, None, :, None])
    matches = matches & live_slots[None, :, None, :] & enabled[:, None, None, None]
    strips = jnp.einsum(
        "mnkp,npxy->mxnky", matches.astype(jnp.bfloat16), stored, preferred_element_type=jnp.float32
    )
    return strips.reshape(targets.shape[0], width, sources * per_source * width)


def per_device(blocks, slot_rows, slot_cols, counts, col_window):
    gathered = (
        lax.all_gather(blocks, "col", axis=1, tiled=True),
        lax.all_gather(slot_rows, "col", axis=1, tiled=True),
        lax.all_gather(slot_cols, "col", axis=1, tiled=True),
        lax.all_gather(counts, "col", axis=1, tiled=True),
    )
    panel_store = gathered[0][0]
    panel_rows = gathered[1][0]
    panel_cols = gathered[2][0]
    panel_counts = gathered[3][0]
    window_rows = jnp.arange(RL)
    left_strip = build_strips(
        panel_store, panel_rows, panel_cols, panel_counts, window_rows, window_rows >= 0
    ).astype(jnp.bfloat16)
    group_size = lax.axis_size("row") // lax.axis_size("col")
    window = col_window[0]
    owner_part = window // RL
    owner_slot = window % RL
    strip_total = jnp.zeros(
        (window.shape[0], left_strip.shape[1], left_strip.shape[2]), jnp.float32
    )
    for source in range(group_size):
        root_index = lax.axis_index("col") * group_size + source
        received = (
            broadcast(gathered[0], "row", root_index),
            broadcast(gathered[1], "row", root_index),
            broadcast(gathered[2], "row", root_index),
            broadcast(gathered[3], "row", root_index),
        )
        strip_total = strip_total + build_strips(
            received[0][0],
            received[1][0],
            received[2][0],
            received[3][0],
            owner_slot,
            owner_part == source,
        )
    right_strip = strip_total.astype(jnp.bfloat16)
    return jnp.einsum("axk,byk->abxy", left_strip, right_strip, preferred_element_type=jnp.float32)


def solution(mesh):
    placed = (
        P("row", "col", None, None, None),
        P("row", "col", None),
        P("row", "col", None),
        P("row", "col"),
        P("col", None),
    )
    return jax.shard_map(
        per_device,
        mesh=mesh,
        in_specs=placed,
        out_specs=P("row", "col", None, None),
        check_vma=False,
    )
```

profile of v0, /device:TPU:1, one launch (start us, length us, event | category | flops | bytes accessed | tf_op | source)
XLA Modules:
  0.0 566.5 jit_solution(14841405505928219722)
XLA Ops:
  6.5 0.7 all-gather.2.cloned.1.call-update
  7.3 98.7 %all-gather.2.cloned.1.call-done = bf16[1,8,16,128,128]{4,3,2,0,1:T(8,128)(2,1)} async-done(((bf16[1,1,16,128,128]{4,3,2,0,1:T(8,128)(2,1)}), bf16[1,8,16,128,128]{4,3,2,0,1:T(8,128)(2,1)}) %all-gather.2.cloned.1.call-update) | async-done | bytes 4194320 | tf_op jit(solution)/shard_map/all_gather | solution.py:33
  106.0 7.5 %select_bitcast_fusion.3 = (bf16[8,16,128,128]{3,2,1,0:T(8,128)(2,1)}, bf16[8,16,128,128]{3,2,1,0:T(8,128)(2,1)}, bf16[8,16,128,128]{3,2,1,0:T(8,128)(2,1)}, bf16[8,16,128,128]{3,2,1,0:T(8,128)(2,1)}) fusion(bf16[1,8,16,128,128]{4,3,2,0,1:T(8,128)(2,1)} %all-gather.2.cloned.1.call-done, pred[]{:T(512)S(6)} %eq.248, pred[]{:T(512)S(6)} %eq.276, pred[]{:T(512)S(6)} %eq.267, ...), kind=kLoop, calls=%fused_computation.16 | loop fusion | flops 8388608 | bytes 20971524 | tf_op jit(solution)/shard_map/squeeze | solution.py:62
  114.2 0.6 dynamic-slice
  114.8 0.7 bitcast_dynamic-update-slice_fusion
  115.5 8.0 %all-reduce = s32[8]{0:T(128)S(1)} all-reduce(s32[8]{0:T(128)S(1)} %bitcast_dynamic-update-slice_fusion), channel_id=1, replica_groups=mesh['row'=32,'col'=8] {'col'}, use_global_device_ids=true, to_apply=%add | all-reduce | flops 8 | bytes 64
  123.5 14.0 %all_gather.13 = s32[1,8,16]{2,0,1:T(1,128)S(1)} all-gather(s32[1,1,16]{2,0,1:T(1,128)S(1)} %bitcast.102), channel_id=1, replica_groups=mesh['row'=32,'col'=8] {'col'}, dimensions={1}, use_global_device_ids=true | all-gather | bytes 576 | tf_op jit(solution)/shard_map/all_gather | solution.py:34
  137.5 13.1 %all_gather.14 = s32[1,8,16]{2,0,1:T(1,128)S(1)} all-gather(s32[1,1,16]{2,0,1:T(1,128)S(1)} %bitcast.103), channel_id=1, replica_groups=mesh['row'=32,'col'=8] {'col'}, dimensions={1}, use_global_device_ids=true | all-gather | bytes 576 | tf_op jit(solution)/shard_map/all_gather | solution.py:35
  150.6 162.4 %all-reduce.1 = (s32[8]{0:T(128)S(1)}, s32[8,16]{1,0:T(8,128)S(1)}, s32[8,16]{1,0:T(8,128)S(1)}, s32[8]{0:T(128)S(1)}, s32[8,16]{1,0:T(8,128)S(1)}, /*index=5*/s...) all-reduce(s32[8]{0:T(128)S(1)} %get-tuple-element.45, ...), channel_id=1, replica_groups=mesh['row'=32,'col'=8] {'row'}, use_global_device_ids=true, to_apply=%region_15.16 | all-reduce | flops 1056 | bytes 8448 | tf_op jit(solution)/shard_map/psum | solution.py:12
  313.0 0.1 iota_compare_fusion.6
  313.1 0.1 iota_compare_fusion.7
  313.2 0.1 iota_compare_fusion.8
  313.2 0.1 iota_compare_fusion.9
  313.4 0.1 broadcast_compare_fusion.3
  313.5 0.1 and_bitcast_fusion.1
  313.6 0.1 and_bitcast_fusion
  313.7 10.9 %fusion.3 = bf16[8,20,2,128,128]{4,1,3,2,0:T(8,128)(2,1)} fusion(bf16[8,16,128,128,1]{3,2,1,0,4:T(8,128)(2,1)} %bitcast.92, pred[20,8,2,16,1]{3,2,1,0,4:T(4,128)(4,1)S(1)} %and_bitcast_fusion), kind=kOutput, calls=%fused_computation.3 | convolution fusion | flops 167772160 | bytes 14685184 | tf_op jit(solution)/shard_map/mnkp,npxy->mxnky/dot_general | solution.py:25
  324.7 209.4 %all-reduce.5.cloned.1.call-done = (bf16[8,16,128,128]{3,2,1,0:T(8,128)(2,1)}, bf16[8,16,128,128]{3,2,1,0:T(8,128)(2,1)}, bf16[8,16,128,128]{3,2,1,0:T(8,128)(2,1)}, bf16[8,16,128,128]{3,2,1,0:T(8,128)(2,1)}) async-done(((bf16[8,16,128,128]{3,2,1,0:T(8,128)(2,1)}, bf16[8,16,128,128]{3,2,1,0:T(8,128)(2,1)}, bf16[8,16,128,128]{3,2,1,0:T(8,128)(2,1)}, bf16[8,16,128,128]{3,2,1,0:T(8,128)(2,1)}), ...) | async-done | bytes 16777232 | tf_op jit(solution)/shard_map/psum | solution.py:12
  534.1 5.1 fusion.7
  539.2 2.8 fusion.5
  542.0 2.8 fusion.9
  544.9 4.2 fusion.11
  549.0 8.5 %fusion.14 = f32[20,2,128,128]{2,3,0,1:T(8,128)S(1)} fusion(bf16[8,20,2,128,128]{4,1,3,2,0:T(8,128)(2,1)} %fusion.3, f32[8,128,128,2,2]{2,4,3,1,0:T(2,128)S(1)} %fusion.5, f32[8,128,128,2,2]{2,4,3,1,0:T(2,128)S(1)} %fusion.7, f32[8,128,128,2,2]{2,4,3,1,0:T(2,128)S(1)} %fusion.9, f32[8,128,128,2,2]{2,4,3,1,0:T(2,128)} %fusion.11), kind=kOutput, calls=%fused_computation.21 | convolution fusion | flops 2686451712 | bytes 21495808 | tf_op jit(solution)/shard_map/axk,byk->abxy/dot_general | solution.py:70
  557.6 2.1 copy.18
  (29 shorter events, 0.2 us)
Async XLA Ops:
  6.5 99.5 %all-gather.2.cloned.1.call-start = ((), (), s32[]{:S(2)}) async-start(), calls=%async_computation | async-start | bytes 4718592 | tf_op jit(solution)/shard_map/all_gather | solution.py:33
  7.3 526.8 %all-reduce.5.cloned.1.call-start = ((), (), s32[]{:S(2)}) async-start(), calls=%async_computation.1 | async-start | bytes 33554432 | tf_op jit(solution)/shard_map/psum | solution.py:12
  113.5 0.7 copy-start.6
  113.5 10.0 %copy-start.3 = (s32[1,1,16]{2,1,0:T(1,128)S(1)}, s32[1,1,16]{2,1,0:T(1,128)}, u32[]{:S(2)}) copy-start(s32[1,1,16]{2,1,0:T(1,128)} %param.6) | copy-start | bytes 196
  113.5 24.0 %copy-start.4 = (s32[1,1,16]{2,1,0:T(1,128)S(1)}, s32[1,1,16]{2,1,0:T(1,128)}, u32[]{:S(2)}) copy-start(s32[1,1,16]{2,1,0:T(1,128)} %param.7) | copy-start | bytes 196
  113.5 199.5 %copy-start.5 = (s32[1,2]{1,0:T(1,128)S(1)}, s32[1,2]{1,0:T(1,128)}, u32[]{:S(2)}) copy-start(s32[1,2]{1,0:T(1,128)} %param.9) | copy-start | bytes 28
  534.1 5.1 copy-start
  539.2 2.8 copy-start.2
  542.0 2.9 copy-start.1
Sparse Core Ops, SparseCore 0:
  9.1 96.8 all-gather.1
  113.7 420.3 all-reduce.4
where the time goes:
time: 573 us; the launch traced here: 566 us
  waiting for transfers between devices  309 us (54%)
  blocking collectives  197 us (34%)
  matrix products  34.3 us (6%)
  between operations  14.2 us (2%)
  other arithmetic  8.15 us (1%)
    psum x1, waiting for transfers between devices, broadcast(): return lax.psum(kept, axis)  209 us
    psum x1, blocking collectives, broadcast(): return lax.psum(kept, axis)  162 us
    all_gather x1, waiting for transfers between devices, per_device(): lax.all_gather(blocks, 'col', axis=1, tiled=True)  98.7 us
    dot_general x5, matrix products, build_strips(): jnp.einsum('mnkp,npxy->mxnky', matches.astype(jnp.bfloat16), stored, pref...  25.8 us
    all_gather x1, blocking collectives, per_device(): lax.all_gather(slot_rows, 'col', axis=1, tiled=True)  14 us
    all_gather x1, blocking collectives, per_device(): lax.all_gather(slot_cols, 'col', axis=1, tiled=True)  13.1 us
  transfers between devices with their start and end apart: 2, of which 2 were waited for; matrix products, arithmetic and copies ran while one was open for 2% of the time, Pallas kernels for 0%

commit v1 on v0

v1 whole, which is shorter than its diff:
```python
import jax
import jax.numpy as jnp
from jax import lax
from jax.experimental import pallas as pl
from jax.experimental.pallas import tpu as pltpu
from jax.sharding import PartitionSpec as P

MESH = pl.DeviceIdType.MESH
BLK = 128
RL = 20
SLOTS = 16
NONE = SLOTS
COLS = 8
WINDOW_LANE = 64

CHUNKS = {"ZA": (0, 5), "ZB": (5, 5), "XA": (10, 3), "XB": (13, 3)}
SOURCES = ((0, 0), (0, 1), (-1, 0), (1, 0), (2, 0), (-1, 1), (1, 1), (2, 1))
ROWS_AT_ONCE = 5


def kernel(
    blocks_ref, rows_ref, cols_ref, counts_ref, window_ref, out_ref,
    own, store_1, store_2, store_3, store_4, store_5, store_6, store_7,
    meta, table, picked, offered, right,
    left_send, left_recv, meta_send, meta_recv, offer_send, offer_recv, spread_send, spread_recv, local_sem,
):
    r = lax.axis_index("row")
    c = lax.axis_index("col")
    zh, y, k = r // 8, lax.rem(r // 2, 4), lax.rem(r, 2)
    x, zl = c // 2, lax.rem(c, 2)
    store = dict(zip(SOURCES, (own, store_1, store_2, store_3, store_4, store_5, store_6, store_7)))

    def column_of(dx, dz):
        return lax.rem(x + (dx + 4), 4) * 2 + (zl if dz == 0 else 1 - zl)

    to_right, to_left, to_pair = column_of(1, 0), column_of(-1, 0), column_of(0, 1)
    target, part = r // 4, lax.rem(r, 4)
    offer_rows = [4 * lax.rem(c + 1, COLS) + t for t in range(4)]
    offering = lax.rem(r // 4 + (COLS - 1), COLS)

    load_own = pltpu.make_async_copy(blocks_ref.at[0, 0], own.at[pl.ds(0, SLOTS)], local_sem.at[0])
    load_own.start()

    barrier = pltpu.get_barrier_semaphore()
    senders = [(r, lax.rem(c + o, COLS)) for o in range(1, COLS)]
    senders += [(4 * c + g, offering) for g in range(4)]
    senders += [(lax.rem(zh + o, 4) * 8 + y * 2 + k, c) for o in range(1, 4)]
    senders += [(zh * 8 + lax.rem(y + o, 4) * 2 + k, c) for o in range(1, 4)]
    senders += [(zh * 8 + y * 2 + 1 - k, c)]
    for sender in senders:
        pl.semaphore_signal(barrier, inc=1, device_id=sender, device_id_type=MESH)

    lane = lax.broadcasted_iota(jnp.int32, (8, 128), 1)
    found = jnp.full((8, 128), NONE, jnp.int32)
    live = counts_ref[0, 0]
    for s in range(SLOTS):
        position = jnp.where(s < live, rows_ref[0, 0, s] * 2 + cols_ref[0, 0, s], 127)
        found = jnp.where(lane == position, s, found)
    for b in range(2):
        found = jnp.where(lane == WINDOW_LANE + b, window_ref[0, b], found)
    meta[0] = found
    for source in SOURCES:
        store[source][NONE] = jnp.zeros((BLK, BLK), jnp.bfloat16)

    pl.semaphore_wait(barrier, len(senders))

    started = []

    def send(src, dst, send_sem, recv_sem, device):
        copy = pltpu.make_async_remote_copy(
            src_ref=src, dst_ref=dst, send_sem=send_sem, recv_sem=recv_sem, device_id=device, device_id_type=MESH
        )
        copy.start()
        started.append(copy)
        return copy

    left = {}

    def send_left(source, chunk, column, lands):
        first, size = CHUNKS[chunk]
        sem = len(left)
        left[(lands, chunk)] = send(
            store[source].at[pl.ds(first, size)], store[lands].at[pl.ds(first, size)],
            left_send.at[sem], left_recv.at[sem], (r, column),
        )

    meta_copies = [
        send(meta.at[0], meta.at[o], meta_send.at[o], meta_recv.at[o], (r, lax.rem(c + o, COLS)))
        for o in range(1, COLS)
    ]
    load_own.wait()
    send_left((0, 0), "ZA", to_pair, (0, 1))
    send_left((0, 0), "XA", to_right, (-1, 0))
    send_left((0, 0), "XB", to_left, (1, 0))
    send_left((0, 0), "XB", to_right, (-1, 0))
    send_left((0, 0), "XA", to_left, (1, 0))

    for copy in meta_copies:
        copy.wait_recv()
    load_table = pltpu.make_async_copy(meta, table, local_sem.at[1])
    load_table.start()
    load_table.wait()

    window_source = lax.rem(c - target + COLS, COLS)
    for b in range(2):
        row = table[window_source, 0, WINDOW_LANE + b] - part * RL
        mine = (row >= 0) & (row < RL)
        for j in range(2):
            place = jnp.where(mine, row, 0) * 2 + j
            slot = jnp.where(mine, table[0, 0, place], NONE)
            picked[2 * b + j] = own[slot]
    for t in range(4):
        send(picked.at[t], offered.at[part], offer_send.at[t], offer_recv.at[part], (offer_rows[t], target))

    send_left((0, 0), "ZB", to_pair, (0, 1))
    send_left((0, 0), "ZA", to_right, (-1, 0))
    send_left((0, 0), "ZB", to_left, (1, 0))
    send_left((0, 0), "ZB", to_right, (-1, 0))
    send_left((0, 0), "ZA", to_left, (1, 0))
    send_left((0, 0), "XA", to_pair, (0, 1))
    send_left((0, 0), "XB", to_pair, (0, 1))

    def arrived(lands, *chunks):
        for chunk in chunks:
            left[(lands, chunk)].wait_recv()

    for g in range(4):
        pltpu.make_async_remote_copy(
            src_ref=picked.at[g], dst_ref=offered.at[g], send_sem=offer_send.at[g], recv_sem=offer_recv.at[g],
            device_id=(offer_rows[0], target), device_id_type=MESH,
        ).wait_recv()
    total = offered[0].astype(jnp.float32)
    for g in range(1, 4):
        total = total + offered[g].astype(jnp.float32)
    lane_yk = y * 2 + k
    right[lane_yk, zh] = total.astype(jnp.bfloat16)
    z_copies = [
        send(
            right.at[lane_yk, zh], right.at[lane_yk, zh], spread_send.at[o], spread_recv.at[o],
            (lax.rem(zh + o, 4) * 8 + y * 2 + k, c),
        )
        for o in range(1, 4)
    ]

    arrived((-1, 0), "XA")
    send_left((-1, 0), "XA", to_right, (2, 0))
    arrived((1, 0), "XB")
    send_left((1, 0), "XB", to_left, (2, 0))
    send_left((-1, 0), "XA", to_pair, (-1, 1))
    send_left((1, 0), "XB", to_pair, (1, 1))
    arrived((0, 1), "ZA")
    send_left((0, 1), "ZA", to_right, (-1, 1))
    send_left((0, 1), "ZA", to_left, (1, 1))

    for copy in z_copies:
        copy.wait_recv()
    y_copies = [
        send(
            right.at[lane_yk], right.at[lane_yk], spread_send.at[4 + o], spread_recv.at[4 + o],
            (zh * 8 + lax.rem(y + o, 4) * 2 + k, c),
        )
        for o in range(1, 4)
    ]

    def send_core(o):
        slab = lax.rem(y + (4 - o), 4) * 2 + k
        return send(
            right.at[slab], right.at[slab], spread_send.at[8 + o], spread_recv.at[8 + o], (zh * 8 + y * 2 + 1 - k, c)
        )

    core_copies = [send_core(0)]

    arrived((-1, 0), "XB")
    send_left((-1, 0), "XB", to_pair, (-1, 1))
    arrived((1, 0), "XA")
    send_left((1, 0), "XA", to_pair, (1, 1))
    arrived((0, 1), "ZB")
    send_left((0, 1), "ZB", to_left, (1, 1))
    send_left((0, 1), "ZB", to_right, (-1, 1))
    arrived((-1, 0), "ZA")
    send_left((-1, 0), "ZA", to_right, (2, 0))
    arrived((1, 0), "ZB")
    send_left((1, 0), "ZB", to_left, (2, 0))
    arrived((2, 0), "XA", "XB")
    send_left((2, 0), "XA", to_pair, (2, 1))
    send_left((2, 0), "XB", to_pair, (2, 1))

    for o in (1, 3, 2):
        y_copies[o - 1].wait_recv()
        core_copies.append(send_core(o))

    arrived((-1, 1), "ZA")
    send_left((-1, 1), "ZA", to_right, (2, 1))
    arrived((1, 1), "ZB")
    send_left((1, 1), "ZB", to_left, (2, 1))

    for copy in core_copies:
        copy.wait_recv()

    def multiply(source, first):
        column = column_of(*source)
        entry = lax.rem(c - column + COLS, COLS)
        holder = lax.rem(column + 1, COLS)
        slab, depth = 4 * lax.rem(holder, 2), holder // 2
        factor = jnp.concatenate(
            [
                jnp.concatenate([right[slab + 2 * b + j, depth] for j in range(2)], axis=1)
                for b in range(2)
            ],
            axis=0,
        )

        def some_rows(step, carry):
            strips = []
            for a in range(ROWS_AT_ONCE):
                place = (step * ROWS_AT_ONCE + a) * 2
                strips.append(
                    jnp.concatenate([store[source][table[entry, 0, place + j]] for j in range(2)], axis=1)
                )
            product = lax.dot_general(
                jnp.concatenate(strips, axis=0), factor, (((1,), (1,)), ((), ())), preferred_element_type=jnp.float32
            )
            for a in range(ROWS_AT_ONCE):
                for b in range(2):
                    piece = product[a * BLK:(a + 1) * BLK, b * BLK:(b + 1) * BLK]
                    if first:
                        out_ref[step * ROWS_AT_ONCE + a, b] = piece
                    else:
                        out_ref[step * ROWS_AT_ONCE + a, b] += piece
            return carry

        lax.fori_loop(0, RL // ROWS_AT_ONCE, some_rows, 0)

    waits = {
        (0, 0): (),
        (0, 1): ("XA", "XB"),
        (-1, 0): ("ZB",),
        (1, 0): ("ZA",),
        (2, 0): ("ZA", "ZB"),
        (-1, 1): ("ZB", "XA", "XB"),
        (1, 1): ("ZA", "XA", "XB"),
        (2, 1): ("ZA", "ZB", "XA", "XB"),
    }
    for source in SOURCES:
        arrived(source, *waits[source])
        multiply(source, source == (0, 0))

    for copy in started:
        copy.wait_send()


def per_device(blocks, slot_rows, slot_cols, counts, col_window):
    hbm = pl.BlockSpec(memory_space=pl.ANY)
    scalars = pl.BlockSpec(memory_space=pltpu.SMEM)
    dma = pltpu.SemaphoreType.DMA
    return pl.pallas_call(
        kernel,
        out_shape=jax.ShapeDtypeStruct((RL, 2, BLK, BLK), jnp.float32),
        in_specs=[hbm, scalars, scalars, scalars, scalars],
        out_specs=pl.BlockSpec(memory_space=pltpu.VMEM),
        scratch_shapes=[
            *[pltpu.VMEM((SLOTS + 1, BLK, BLK), jnp.bfloat16) for _ in SOURCES],
            pltpu.VMEM((COLS, 8, 128), jnp.int32),
            pltpu.SMEM((COLS, 8, 128), jnp.int32),
            pltpu.VMEM((4, BLK, BLK), jnp.bfloat16),
            pltpu.VMEM((4, BLK, BLK), jnp.bfloat16),
            pltpu.VMEM((8, 4, BLK, BLK), jnp.bfloat16),
            dma((28,)), dma((28,)), dma((8,)), dma((8,)), dma((4,)), dma((4,)), dma((12,)), dma((12,)), dma((2,)),
        ],
        compiler_params=pltpu.CompilerParams(
            collective_id=0, has_side_effects=True, vmem_limit_bytes=24 * 1024 * 1024
        ),
        cost_estimate=pl.CostEstimate(flops=2 * RL * BLK * 2048 * 256, bytes_accessed=8 * 1024 * 1024, transcendentals=0),
    )(blocks, slot_rows, slot_cols, counts, col_window)


def solution(mesh):
    placed = (
        P("row", "col", None, None, None),
        P("row", "col", None),
        P("row", "col", None),
        P("row", "col"),
        P("col", None),
    )
    return jax.shard_map(
        per_device, mesh=mesh, in_specs=placed, out_specs=P("row", "col", None, None), check_vma=False
    )
```

time: 573 us -> 58.8 us (0.10); the launches traced: 566 us -> 58.6 us
  waiting for transfers between devices: 309 us -> 0 us
  blocking collectives: 197 us -> 0 us
  Pallas kernels: 0 us -> 53.5 us
  matrix products: 34.3 us -> 0 us
  between operations: 14.2 us -> 0.67 us
  other arithmetic: 8.15 us -> 0 us
    psum x1 -> x0, waiting for transfers between devices: 209 us -> none  [broadcast(): return lax.psum(kept, axis)]
    psum x1 -> x0, blocking collectives: 162 us -> none  [broadcast(): return lax.psum(kept, axis)]
    all_gather x1 -> x0, waiting for transfers between devices: 98.7 us -> none  [per_device(): lax.all_gather(blocks, 'col', axis=1, tiled=True)]
    pallas_call x0 -> x1, Pallas kernels: none -> 53.5 us  [per_device(): pl.pallas_call(kernel, out_shape=jax.ShapeDtypeStruct((RL, 2, BLK, BLK),...]
    dot_general x6 -> x0, matrix products: 34.3 us -> none  [the longest x5 25.8 us: build_strips(): jnp.einsum('mnkp,npxy->mxnky', matches.astype(jnp.bfloat16), stored, pref...]
    all_gather x2 -> x0, blocking collectives: 27.1 us -> none  [the longest x1 14 us: per_device(): lax.all_gather(slot_rows, 'col', axis=1, tiled=True)]
    unnamed x1 -> x0, blocking collectives: 8.01 us -> none
    squeeze x1 -> x0, other arithmetic: 7.46 us -> none  [per_device(): received[0][0]]
  transfers between devices with their start and end apart: 2 -> 0, of which waited for: 2 -> 0; matrix products, arithmetic and copies ran while one was open for 2% -> 0% of each run, Pallas kernels for 0% -> 0%
where the time goes in v1:
time: 58.8 us; the launch traced here: 58.6 us
  Pallas kernels  53.5 us (91%)
  local copies, waits for them, and re-layouts  4.49 us (8%)
  between operations  0.67 us (1%)
    pallas_call x1, Pallas kernels, per_device(): pl.pallas_call(kernel, out_shape=jax.ShapeDtypeStruct((RL, 2, BLK, BLK),...  53.5 us
    unnamed x9, local copies, waits for them, and re-layouts  4.49 us

profile of v1, /device:TPU:1, one launch (start us, length us, event | category | flops | bytes accessed | tf_op | source)
XLA Modules:
  0.0 58.6 jit_solution(12053369133389021870)
XLA Ops:
  0.7 0.0 copy-start
  0.7 1.0 %copy-done = bf16[1,1,16,128,128]{4,3,2,1,0:T(8,128)(2,1)S(1)} copy-done((bf16[1,1,16,128,128]{4,3,2,1,0:T(8,128)(2,1)S(1)}, bf16[1,1,16,128,128]{4,3,2,1,0:T(8,128)(2,1)}, u32[]{:S(2)}) %copy-start) | copy-done | bytes 524312
  1.7 0.0 copy-start.1
  1.7 0.7 %copy-done.1 = s32[1,1,16]{2,1,0:T(1,128)S(1)} copy-done((s32[1,1,16]{2,1,0:T(1,128)S(1)}, s32[1,1,16]{2,1,0:T(1,128)}, u32[]{:S(2)}) %copy-start.1) | copy-done | bytes 88
  2.4 0.0 copy-start.2
  2.4 0.7 %copy-done.2 = s32[1,1,16]{2,1,0:T(1,128)S(1)} copy-done((s32[1,1,16]{2,1,0:T(1,128)S(1)}, s32[1,1,16]{2,1,0:T(1,128)}, u32[]{:S(2)}) %copy-start.2) | copy-done | bytes 88
  3.0 0.0 copy-start.3
  3.0 0.7 %copy-done.3 = s32[1,2]{1,0:T(1,128)S(1)} copy-done((s32[1,2]{1,0:T(1,128)S(1)}, s32[1,2]{1,0:T(1,128)}, u32[]{:S(2)}) %copy-start.3) | copy-done | bytes 32
  3.7 53.5 %shard_map.55 = f32[20,2,128,128]{3,2,1,0:T(8,128)S(1)} custom-call(bf16[1,1,16,128,128]{4,3,2,1,0:T(8,128)(2,1)S(1)} %copy-done, s32[1,1,16]{2,1,0:T(1,128)S(1)} %copy-done.1, s32[1,1,16]{2,1,0:T(1,128)S(1)} %copy-done.2, s32[1,1]{1,0:T(1,128)S(6)} %copy.7.counts_ref, s32[1,2]{1,0:T(1,128)S(1)} %copy-done.3), custom_call_target="tpu_custom_call" | custom-call | flops 2684354560 | bytes 8388608 | tf_op jit(solution)/shard_map/pallas_call | solution.py:256
  57.1 1.5 %copy.8 = f32[20,2,128,128]{3,2,1,0:T(8,128)} copy(f32[20,2,128,128]{3,2,1,0:T(8,128)S(1)} %shard_map.55) | data formatting | bytes 5242880
Async XLA Ops:
  0.7 1.0 %copy-start = (bf16[1,1,16,128,128]{4,3,2,1,0:T(8,128)(2,1)S(1)}, bf16[1,1,16,128,128]{4,3,2,1,0:T(8,128)(2,1)}, u32[]{:S(2)}) copy-start(bf16[1,1,16,128,128]{4,3,2,1,0:T(8,128)(2,1)} %blocks_ref.1) | copy-start | bytes 1572868
  1.7 0.7 %copy-start.1 = (s32[1,1,16]{2,1,0:T(1,128)S(1)}, s32[1,1,16]{2,1,0:T(1,128)}, u32[]{:S(2)}) copy-start(s32[1,1,16]{2,1,0:T(1,128)} %rows_ref.1) | copy-start | bytes 196
  2.4 0.7 %copy-start.2 = (s32[1,1,16]{2,1,0:T(1,128)S(1)}, s32[1,1,16]{2,1,0:T(1,128)}, u32[]{:S(2)}) copy-start(s32[1,1,16]{2,1,0:T(1,128)} %cols_ref.1) | copy-start | bytes 196
  3.0 0.7 %copy-start.3 = (s32[1,2]{1,0:T(1,128)S(1)}, s32[1,2]{1,0:T(1,128)}, u32[]{:S(2)}) copy-start(s32[1,2]{1,0:T(1,128)} %window_ref.1) | copy-start | bytes 28

commit v2 on v1

v2 whole, which is shorter than its diff:
```python
import jax
import jax.numpy as jnp
from jax import lax
from jax.experimental import pallas as pl
from jax.experimental.pallas import tpu as pltpu
from jax.sharding import PartitionSpec as P

MESH = pl.DeviceIdType.MESH
BLK = 128
RL = 20
SLOTS = 16
NONE = SLOTS
COLS = 8

CHUNKS = {"ZA": (0, 5), "ZB": (5, 5), "XA": (10, 3), "XB": (13, 3)}
SOURCES = ((0, 0), (0, 1), (-1, 0), (1, 0), (2, 0), (-1, 1), (1, 1), (2, 1))


def kernel(
    blocks_ref, rows_ref, cols_ref, window_ref, counts_ref, out_ref,
    own, store_1, store_2, store_3, store_4, store_5, store_6, store_7,
    rows, cols, window, meta, table, own_table, picked, given, mixed, offered, right,
    left_send, left_recv, meta_send, meta_recv, window_send, window_recv, pick_send, pick_recv,
    offer_send, offer_recv, spread_send, spread_recv, local_sem,
):
    r = lax.axis_index("row")
    c = lax.axis_index("col")
    zh, y, k = r // 8, lax.rem(r // 2, 4), lax.rem(r, 2)
    x, zl = c // 2, lax.rem(c, 2)
    store = dict(zip(SOURCES, (own, store_1, store_2, store_3, store_4, store_5, store_6, store_7)))

    def row_of(zh, y, k):
        return zh * 8 + y * 2 + k

    def column_of(dx, dz):
        return lax.rem(x + (dx + 4), 4) * 2 + (zl if dz == 0 else 1 - zl)

    to_right, to_left, to_pair = column_of(1, 0), column_of(-1, 0), column_of(0, 1)
    mates = [(r, lax.rem(c + o, COLS)) for o in range(1, COLS)]
    z_mates = [(row_of(lax.rem(zh + o, 4), y, k), c) for o in range(1, 4)]
    y_mates = [(row_of(zh, lax.rem(y + o, 4), k), c) for o in range(1, 4)]
    other_core = (row_of(zh, y, 1 - k), c)
    target, part = r // 4, lax.rem(r, 4)
    offer_rows = [row_of(lax.rem(x + 2, 4), 2 * (1 - zl) + b, k) for b in range(2)]
    offer_senders = [(4 * c + 2 * g + k, lax.rem(zh + 2, 4) * 2 + 1 - y // 2) for g in range(2)]

    barrier = pltpu.get_barrier_semaphore()
    senders = mates + z_mates + y_mates + [other_core] + offer_senders
    for sender in senders:
        pl.semaphore_signal(barrier, inc=1, device_id=sender, device_id_type=MESH)

    loads = [
        pltpu.make_async_copy(src, dst, local_sem.at[i])
        for i, (src, dst) in enumerate(
            [(rows_ref, rows), (cols_ref, cols), (blocks_ref.at[0, 0], own.at[pl.ds(0, SLOTS)])]
        )
    ]
    for load in loads:
        load.start()
    for source in SOURCES:
        store[source][NONE] = jnp.zeros((BLK, BLK), jnp.bfloat16)
    for load in loads[:2]:
        load.wait()

    lane = lax.broadcasted_iota(jnp.int32, (8, 128), 1)
    found = jnp.full((8, 128), NONE, jnp.int32)
    live = counts_ref[0, 0]
    for s in range(SLOTS):
        position = jnp.where(s < live, rows[0, 0, s] * 2 + cols[0, 0, s], 127)
        found = jnp.where(lane == position, s, found)
    meta[0] = found
    load_own_table = pltpu.make_async_copy(meta.at[0], own_table, local_sem.at[3])
    load_own_table.start()
    load_own_table.wait()
    loads[2].wait()

    pl.semaphore_wait(barrier, len(senders))

    started = []

    def copy_to(src, dst, send_sem, recv_sem, device):
        return pltpu.make_async_remote_copy(
            src_ref=src, dst_ref=dst, send_sem=send_sem, recv_sem=recv_sem, device_id=device, device_id_type=MESH
        )

    def send(*what):
        copy = copy_to(*what)
        copy.start()
        started.append(copy)
        return copy

    left = {}

    def send_left(source, chunk, column, lands):
        first, size = CHUNKS[chunk]
        sem = len(left)
        left[(lands, chunk)] = send(
            store[source].at[pl.ds(first, size)], store[lands].at[pl.ds(first, size)],
            left_send.at[sem], left_recv.at[sem], (r, column),
        )

    def arrived(lands, *chunks):
        for chunk in chunks:
            left[(lands, chunk)].wait_recv()

    window_copies = [
        copy_to(window_ref, window, window_send.at[o], window_recv.at[0], mates[o]) for o in range(COLS - 1)
    ]
    home = target == c
    load_window = pltpu.make_async_copy(window_ref, window, local_sem.at[4])

    @pl.when(home)
    def _():
        load_window.start()
        for copy in window_copies:
            copy.start()

    send_left((0, 0), "ZA", to_pair, (0, 1))
    send_left((0, 0), "XA", to_right, (-1, 0))
    send_left((0, 0), "XB", to_left, (1, 0))
    send_left((0, 0), "XB", to_right, (-1, 0))
    send_left((0, 0), "XA", to_left, (1, 0))

    @pl.when(home)
    def _():
        load_window.wait()

    @pl.when(jnp.logical_not(home))
    def _():
        window_copies[0].wait_recv()

    for b in range(2):
        row = window[0, b] - part * RL
        mine = (row >= 0) & (row < RL)
        for j in range(2):
            place = jnp.where(mine, row, 0) * 2 + j
            picked[j, b] = own[jnp.where(mine, own_table[0, place], NONE)]
    pick_copy = send(picked.at[1 - k], given, pick_send.at[0], pick_recv.at[0], other_core)

    send_left((0, 0), "ZB", to_pair, (0, 1))
    send_left((0, 0), "ZA", to_right, (-1, 0))
    send_left((0, 0), "ZB", to_left, (1, 0))

    def add(one, other):
        return (one.astype(jnp.float32) + other.astype(jnp.float32)).astype(jnp.bfloat16)

    pick_copy.wait_recv()
    place_in_pair = lax.rem(y, 2)
    offer_copies = []
    for b in range(2):
        mixed[b] = add(picked[k, b], given[b])
        send(
            mixed.at[b], offered.at[place_in_pair], offer_send.at[b], offer_recv.at[place_in_pair],
            (offer_rows[b], target),
        )

    meta_copies = [
        send(meta.at[0], meta.at[o + 1], meta_send.at[o], meta_recv.at[o], mates[o]) for o in range(COLS - 1)
    ]
    send_left((0, 0), "ZB", to_right, (-1, 0))
    send_left((0, 0), "ZA", to_left, (1, 0))
    send_left((0, 0), "XA", to_pair, (0, 1))
    send_left((0, 0), "XB", to_pair, (0, 1))

    arrived((-1, 0), "XA")
    send_left((-1, 0), "XA", to_right, (2, 0))
    arrived((1, 0), "XB")
    send_left((1, 0), "XB", to_left, (2, 0))
    send_left((-1, 0), "XA", to_pair, (-1, 1))
    send_left((1, 0), "XB", to_pair, (1, 1))
    arrived((0, 1), "ZA")
    send_left((0, 1), "ZA", to_right, (-1, 1))
    send_left((0, 1), "ZA", to_left, (1, 1))

    for g in range(2):
        copy_to(
            mixed.at[g], offered.at[g], offer_send.at[g], offer_recv.at[g], (offer_rows[g], target)
        ).wait_recv()
    slab = y * 2 + k
    right[slab, zh] = add(offered[0], offered[1])

    def send_right(block, sem, device):
        return send(right.at[block], right.at[block], spread_send.at[sem], spread_recv.at[sem], device)

    z_copies = [send_right((slab, zh), o, z_mates[o]) for o in range(3)]
    y_copies = {}

    def spread_block(step):
        depth = lax.rem(zh + (4 - step), 4)
        for o in range(3):
            y_copies[(step, o)] = send_right((slab, depth), 3 + 3 * step + o, y_mates[o])

    spread_block(0)

    arrived((-1, 0), "XB")
    send_left((-1, 0), "XB", to_pair, (-1, 1))
    arrived((1, 0), "XA")
    send_left((1, 0), "XA", to_pair, (1, 1))
    arrived((0, 1), "ZB")
    send_left((0, 1), "ZB", to_left, (1, 1))
    send_left((0, 1), "ZB", to_right, (-1, 1))

    for step in (1, 3):
        z_copies[step - 1].wait_recv()
        spread_block(step)

    arrived((-1, 0), "ZA")
    send_left((-1, 0), "ZA", to_right, (2, 0))
    arrived((1, 0), "ZB")
    send_left((1, 0), "ZB", to_left, (2, 0))

    z_copies[1].wait_recv()
    spread_block(2)
    core_copies = [send_right(slab, 15, other_core)]

    arrived((2, 0), "XA", "XB")
    send_left((2, 0), "XA", to_pair, (2, 1))
    send_left((2, 0), "XB", to_pair, (2, 1))
    arrived((-1, 1), "ZA")
    send_left((-1, 1), "ZA", to_right, (2, 1))
    arrived((1, 1), "ZB")
    send_left((1, 1), "ZB", to_left, (2, 1))

    for copy in meta_copies:
        copy.wait_recv()
    load_table = pltpu.make_async_copy(meta, table, local_sem.at[5])
    load_table.start()

    for o in (0, 2, 1):
        for step in range(4):
            y_copies[(step, o)].wait_recv()
        core_copies.append(send_right(lax.rem(y + (3 - o), 4) * 2 + k, 16 + o, other_core))
    load_table.wait()
    for copy in core_copies:
        copy.wait_recv()

    def multiply(source, first):
        column = column_of(*source)
        entry = lax.rem(c - column + COLS, COLS)
        depth, base = lax.rem(column // 2 + 2, 4), 4 * (1 - lax.rem(column, 2))
        factor = jnp.concatenate(
            [
                jnp.concatenate([right[base + 2 * b + j, depth] for j in range(2)], axis=1)
                for b in range(2)
            ],
            axis=0,
        )
        strips = [
            jnp.concatenate([store[source][table[entry, 0, 2 * a + j]] for j in range(2)], axis=1) for a in range(RL)
        ]
        product = lax.dot_general(
            jnp.concatenate(strips, axis=0), factor, (((1,), (1,)), ((), ())), preferred_element_type=jnp.float32
        )
        for a in range(RL):
            for b in range(2):
                piece = product[a * BLK:(a + 1) * BLK, b * BLK:(b + 1) * BLK]
                if first:
                    out_ref[a, b] = piece
                else:
                    out_ref[a, b] += piece

    waits = {
        (0, 0): (),
        (0, 1): ("XA", "XB"),
        (-1, 0): ("ZB",),
        (1, 0): ("ZA",),
        (2, 0): ("ZA", "ZB"),
        (-1, 1): ("ZB", "XA", "XB"),
        (1, 1): ("ZA", "XA", "XB"),
        (2, 1): ("ZA", "ZB", "XA", "XB"),
    }
    for source in SOURCES:
        arrived(source, *waits[source])
        multiply(source, source == (0, 0))

    for copy in started:
        copy.wait_send()

    @pl.when(home)
    def _():
        for copy in window_copies:
            copy.wait_send()


def per_device(blocks, slot_rows, slot_cols, counts, col_window):
    operands = [
        pltpu.with_memory_space_constraint(value, pltpu.HBM)
        for value in (blocks, slot_rows, slot_cols, col_window)
    ]
    hbm = pl.BlockSpec(memory_space=pltpu.HBM)
    dma = pltpu.SemaphoreType.DMA
    return pl.pallas_call(
        kernel,
        out_shape=jax.ShapeDtypeStruct((RL, 2, BLK, BLK), jnp.float32),
        in_specs=[hbm] * 4 + [pl.BlockSpec(memory_space=pltpu.SMEM)],
        out_specs=pl.BlockSpec(memory_space=pltpu.VMEM),
        scratch_shapes=[
            *[pltpu.VMEM((SLOTS + 1, BLK, BLK), jnp.bfloat16) for _ in SOURCES],
            pltpu.SMEM(slot_rows.shape, jnp.int32),
            pltpu.SMEM(slot_cols.shape, jnp.int32),
            pltpu.SMEM(col_window.shape, jnp.int32),
            pltpu.VMEM((COLS, 8, 128), jnp.int32),
            pltpu.SMEM((COLS, 8, 128), jnp.int32),
            pltpu.SMEM((8, 128), jnp.int32),
            pltpu.VMEM((2, 2, BLK, BLK), jnp.bfloat16),
            pltpu.VMEM((2, BLK, BLK), jnp.bfloat16),
            pltpu.VMEM((2, BLK, BLK), jnp.bfloat16),
            pltpu.VMEM((2, BLK, BLK), jnp.bfloat16),
            pltpu.VMEM((8, 4, BLK, BLK), jnp.bfloat16),
            dma((28,)), dma((28,)), dma((7,)), dma((7,)), dma((7,)), dma((1,)), dma((1,)), dma((1,)),
            dma((2,)), dma((2,)), dma((19,)), dma((19,)), dma((6,)),
        ],
        compiler_params=pltpu.CompilerParams(
            collective_id=0, has_side_effects=True, vmem_limit_bytes=24 * 1024 * 1024
        ),
        cost_estimate=pl.CostEstimate(flops=2 * RL * BLK * 2048 * 256, bytes_accessed=8 * 1024 * 1024, transcendentals=0),
    )(*operands, counts)


def solution(mesh):
    placed = (
        P("row", "col", None, None, None),
        P("row", "col", None),
        P("row", "col", None),
        P("row", "col"),
        P("col", None),
    )
    return jax.shard_map(
        per_device, mesh=mesh, in_specs=placed, out_specs=P("row", "col", None, None), check_vma=False
    )
```

time: 58.8 us -> 54.2 us (0.922)
  local copies, waits for them, and re-layouts: 4.49 us -> 1.49 us
  Pallas kernels: 53.5 us -> 51.9 us
    unnamed x9 -> x1, local copies, waits for them, and re-layouts: 4.49 us -> 1.49 us
    pallas_call x1, Pallas kernels: 53.5 us -> 51.9 us  [per_device(): pl.pallas_call(kernel, out_shape=jax.ShapeDtypeStruct((RL, 2, BLK, BLK),...]
where the time goes in v2:
time: 54.2 us; the launch traced here: 54.1 us
  Pallas kernels  51.9 us (96%)
  local copies, waits for them, and re-layouts  1.49 us (3%)
  between operations  0.66 us (1%)
    pallas_call x1, Pallas kernels, per_device(): pl.pallas_call(kernel, out_shape=jax.ShapeDtypeStruct((RL, 2, BLK, BLK),...  51.9 us
    unnamed x1, local copies, waits for them, and re-layouts  1.49 us

profile of v2, /device:TPU:1, one launch (start us, length us, event | category | flops | bytes accessed | tf_op | source)
XLA Modules:
  0.0 54.1 jit_solution(14710201377652527225)
XLA Ops:
  0.7 51.9 %shard_map.55 = f32[20,2,128,128]{3,2,1,0:T(8,128)S(1)} custom-call(bf16[1,1,16,128,128]{4,3,2,1,0:T(8,128)(2,1)} %blocks_ref.1, s32[1,1,16]{2,1,0:T(1,128)} %rows_ref.1, s32[1,1,16]{2,1,0:T(1,128)} %cols_ref.1, s32[1,2]{1,0:T(1,128)} %window_ref.1, s32[1,1]{1,0:T(1,128)S(6)} %copy.7.counts_ref), custom_call_target="tpu_custom_call" | custom-call | flops 2684354560 | bytes 8388608 | tf_op jit(solution)/shard_map/pallas_call | solution.py:292
  52.6 1.5 %copy.8 = f32[20,2,128,128]{3,2,1,0:T(8,128)} copy(f32[20,2,128,128]{3,2,1,0:T(8,128)S(1)} %shard_map.55) | data formatting | bytes 5242880

commit v3 on v2

--- a/solution.py
+++ b/solution.py
@@ -19,7 +19,7 @@
 def kernel(
     blocks_ref, rows_ref, cols_ref, window_ref, counts_ref, out_ref,
     own, store_1, store_2, store_3, store_4, store_5, store_6, store_7,
-    rows, cols, window, meta, table, own_table, picked, given, mixed, offered, right,
+    rows, cols, window, meta, table, own_table, picked, given, mixed, right,
     left_send, left_recv, meta_send, meta_recv, window_send, window_recv, pick_send, pick_recv,
     offer_send, offer_recv, spread_send, spread_recv, local_sem,
 ):
@@ -41,11 +41,12 @@
     y_mates = [(row_of(zh, lax.rem(y + o, 4), k), c) for o in range(1, 4)]
     other_core = (row_of(zh, y, 1 - k), c)
     target, part = r // 4, lax.rem(r, 4)
-    offer_rows = [row_of(lax.rem(x + 2, 4), 2 * (1 - zl) + b, k) for b in range(2)]
-    offer_senders = [(4 * c + 2 * g + k, lax.rem(zh + 2, 4) * 2 + 1 - y // 2) for g in range(2)]
+    group = [(4 * target + lax.rem(part + o, 4), c) for o in range(1, 4)]
+    offer_row = row_of(lax.rem(x + 2, 4), 2 * (1 - zl) + part // 2, k)
+    offer_sender = (4 * c + lax.rem(y, 2) * 2 + k, lax.rem(zh + 2, 4) * 2 + 1 - y // 2)
 
     barrier = pltpu.get_barrier_semaphore()
-    senders = mates + z_mates + y_mates + [other_core] + offer_senders
+    senders = mates + z_mates + y_mates + group + [offer_sender] + [other_core]
     for sender in senders:
         pl.semaphore_signal(barrier, inc=1, device_id=sender, device_id_type=MESH)
 
@@ -134,29 +135,26 @@
         mine = (row >= 0) & (row < RL)
         for j in range(2):
             place = jnp.where(mine, row, 0) * 2 + j
-            picked[j, b] = own[jnp.where(mine, own_table[0, place], NONE)]
-    pick_copy = send(picked.at[1 - k], given, pick_send.at[0], pick_recv.at[0], other_core)
+            picked[2 * b + j] = own[jnp.where(mine, own_table[0, place], NONE)]
+    pick_copies = [
+        send(picked.at[lax.rem(part + o, 4)], given.at[o - 1], pick_send.at[o - 1], pick_recv.at[o - 1], group[o - 1])
+        for o in range(1, 4)
+    ]
+    for copy in pick_copies:
+        copy.wait_recv()
+    total = picked[part].astype(jnp.float32)
+    for o in range(3):
+        total = total + given[o].astype(jnp.float32)
+    mixed[...] = total.astype(jnp.bfloat16)
+    slab = y * 2 + k
+    offer_copy = send(mixed, right.at[2 * (2 * (1 - zl) + part // 2) + k, lax.rem(x + 2, 4)], offer_send.at[0], offer_recv.at[0], (offer_row, target))
+    meta_copies = [
+        send(meta.at[0], meta.at[o + 1], meta_send.at[o], meta_recv.at[o], mates[o]) for o in range(COLS - 1)
+    ]
 
     send_left((0, 0), "ZB", to_pair, (0, 1))
     send_left((0, 0), "ZA", to_right, (-1, 0))
     send_left((0, 0), "ZB", to_left, (1, 0))
-
-    def add(one, other):
-        return (one.astype(jnp.float32) + other.astype(jnp.float32)).astype(jnp.bfloat16)
-
-    pick_copy.wait_recv()
-    place_in_pair = lax.rem(y, 2)
-    offer_copies = []
-    for b in range(2):
-        mixed[b] = add(picked[k, b], given[b])
-        send(
-            mixed.at[b], offered.at[place_in_pair], offer_send.at[b], offer_recv.at[place_in_pair],
-            (offer_rows[b], target),
-        )
-
-    meta_copies = [
-        send(meta.at[0], meta.at[o + 1], meta_send.at[o], meta_recv.at[o], mates[o]) for o in range(COLS - 1)
-    ]
     send_left((0, 0), "ZB", to_right, (-1, 0))
     send_left((0, 0), "ZA", to_left, (1, 0))
     send_left((0, 0), "XA", to_pair, (0, 1))
@@ -166,18 +164,10 @@
     send_left((-1, 0), "XA", to_right, (2, 0))
     arrived((1, 0), "XB")
     send_left((1, 0), "XB", to_left, (2, 0))
-    send_left((-1, 0), "XA", to_pair, (-1, 1))
-    send_left((1, 0), "XB", to_pair, (1, 1))
     arrived((0, 1), "ZA")
     send_left((0, 1), "ZA", to_right, (-1, 1))
     send_left((0, 1), "ZA", to_left, (1, 1))
-
-    for g in range(2):
-        copy_to(
-            mixed.at[g], offered.at[g], offer_send.at[g], offer_recv.at[g], (offer_rows[g], target)
-        ).wait_recv()
-    slab = y * 2 + k
-    right[slab, zh] = add(offered[0], offered[1])
+    offer_copy.wait_recv()
 
     def send_right(block, sem, device):
         return send(right.at[block], right.at[block], spread_send.at[sem], spread_recv.at[sem], device)
@@ -192,6 +182,8 @@
 
     spread_block(0)
 
+    send_left((-1, 0), "XA", to_pair, (-1, 1))
+    send_left((1, 0), "XB", to_pair, (1, 1))
     arrived((-1, 0), "XB")
     send_left((-1, 0), "XB", to_pair, (-1, 1))
     arrived((1, 0), "XA")
@@ -199,16 +191,14 @@
     arrived((0, 1), "ZB")
     send_left((0, 1), "ZB", to_left, (1, 1))
     send_left((0, 1), "ZB", to_right, (-1, 1))
-
-    for step in (1, 3):
-        z_copies[step - 1].wait_recv()
-        spread_block(step)
-
     arrived((-1, 0), "ZA")
     send_left((-1, 0), "ZA", to_right, (2, 0))
     arrived((1, 0), "ZB")
     send_left((1, 0), "ZB", to_left, (2, 0))
 
+    for step in (1, 3):
+        z_copies[step - 1].wait_recv()
+        spread_block(step)
     z_copies[1].wait_recv()
     spread_block(2)
     core_copies = [send_right(slab, 15, other_core)]
@@ -302,13 +292,12 @@
             pltpu.VMEM((COLS, 8, 128), jnp.int32),
             pltpu.SMEM((COLS, 8, 128), jnp.int32),
             pltpu.SMEM((8, 128), jnp.int32),
-            pltpu.VMEM((2, 2, BLK, BLK), jnp.bfloat16),
-            pltpu.VMEM((2, BLK, BLK), jnp.bfloat16),
-            pltpu.VMEM((2, BLK, BLK), jnp.bfloat16),
-            pltpu.VMEM((2, BLK, BLK), jnp.bfloat16),
+            pltpu.VMEM((4, BLK, BLK), jnp.bfloat16),
+            pltpu.VMEM((3, BLK, BLK), jnp.bfloat16),
+            pltpu.VMEM((BLK, BLK), jnp.bfloat16),
             pltpu.VMEM((8, 4, BLK, BLK), jnp.bfloat16),
-            dma((28,)), dma((28,)), dma((7,)), dma((7,)), dma((7,)), dma((1,)), dma((1,)), dma((1,)),
-            dma((2,)), dma((2,)), dma((19,)), dma((19,)), dma((6,)),
+            dma((28,)), dma((28,)), dma((7,)), dma((7,)), dma((7,)), dma((1,)), dma((3,)), dma((3,)),
+            dma((1,)), dma((1,)), dma((19,)), dma((19,)), dma((6,)),
         ],
         compiler_params=pltpu.CompilerParams(
             collective_id=0, has_side_effects=True, vmem_limit_bytes=24 * 1024 * 1024

time: 54.2 us -> 50 us (0.923)
  Pallas kernels: 51.9 us -> 47.7 us
    pallas_call x1, Pallas kernels: 51.9 us -> 47.7 us  [per_device(): pl.pallas_call(kernel, out_shape=jax.ShapeDtypeStruct((RL, 2, BLK, BLK),...]
where the time goes in v3:
time: 50 us; the launch traced here: 49.9 us
  Pallas kernels  47.7 us (95%)
  local copies, waits for them, and re-layouts  1.49 us (3%)
  between operations  0.66 us (1%)
    pallas_call x1, Pallas kernels, per_device(): pl.pallas_call(kernel, out_shape=jax.ShapeDtypeStruct((RL, 2, BLK, BLK),...  47.7 us
    unnamed x1, local copies, waits for them, and re-layouts  1.49 us

profile of v3, /device:TPU:1, one launch (start us, length us, event | category | flops | bytes accessed | tf_op | source)
XLA Modules:
  0.0 49.9 jit_solution(16869946147202426989)
XLA Ops:
  0.7 47.7 %shard_map.55 = f32[20,2,128,128]{3,2,1,0:T(8,128)S(1)} custom-call(bf16[1,1,16,128,128]{4,3,2,1,0:T(8,128)(2,1)} %blocks_ref.1, s32[1,1,16]{2,1,0:T(1,128)} %rows_ref.1, s32[1,1,16]{2,1,0:T(1,128)} %cols_ref.1, s32[1,2]{1,0:T(1,128)} %window_ref.1, s32[1,1]{1,0:T(1,128)S(6)} %copy.7.counts_ref), custom_call_target="tpu_custom_call" | custom-call | flops 2684354560 | bytes 8388608 | tf_op jit(solution)/shard_map/pallas_call | solution.py:282
  48.4 1.5 %copy.8 = f32[20,2,128,128]{3,2,1,0:T(8,128)} copy(f32[20,2,128,128]{3,2,1,0:T(8,128)S(1)} %shard_map.55) | data formatting | bytes 5242880

commit v4 on v3

--- a/solution.py
+++ b/solution.py
@@ -35,6 +35,10 @@
     def column_of(dx, dz):
         return lax.rem(x + (dx + 4), 4) * 2 + (zl if dz == 0 else 1 - zl)
 
+    def held_at(column, partner, owner):
+        turned = jnp.where(lax.rem(column + owner, 2) == 0, 1 - partner, partner)
+        return 2 * (1 - lax.rem(column, 2)) + turned
+
     to_right, to_left, to_pair = column_of(1, 0), column_of(-1, 0), column_of(0, 1)
     mates = [(r, lax.rem(c + o, COLS)) for o in range(1, COLS)]
     z_mates = [(row_of(lax.rem(zh + o, 4), y, k), c) for o in range(1, 4)]
@@ -42,8 +46,11 @@
     other_core = (row_of(zh, y, 1 - k), c)
     target, part = r // 4, lax.rem(r, 4)
     group = [(4 * target + lax.rem(part + o, 4), c) for o in range(1, 4)]
-    offer_row = row_of(lax.rem(x + 2, 4), 2 * (1 - zl) + part // 2, k)
-    offer_sender = (4 * c + lax.rem(y, 2) * 2 + k, lax.rem(zh + 2, 4) * 2 + 1 - y // 2)
+    offer_y = held_at(c, part // 2, target)
+    offer_row = row_of(lax.rem(x + 2, 4), offer_y, k)
+    sender_column = lax.rem(zh + 2, 4) * 2 + 1 - y // 2
+    near = jnp.where(lax.rem(sender_column + c, 2) == 0, 1 - lax.rem(y, 2), lax.rem(y, 2))
+    offer_sender = (4 * c + 2 * near + k, sender_column)
 
     barrier = pltpu.get_barrier_semaphore()
     senders = mates + z_mates + y_mates + group + [offer_sender] + [other_core]
@@ -90,7 +97,7 @@
         started.append(copy)
         return copy
 
-    left = {}
+    left, seen = {}, set()
 
     def send_left(source, chunk, column, lands):
         first, size = CHUNKS[chunk]
@@ -102,7 +109,9 @@
 
     def arrived(lands, *chunks):
         for chunk in chunks:
-            left[(lands, chunk)].wait_recv()
+            if (lands, chunk) not in seen:
+                seen.add((lands, chunk))
+                left[(lands, chunk)].wait_recv()
 
     window_copies = [
         copy_to(window_ref, window, window_send.at[o], window_recv.at[0], mates[o]) for o in range(COLS - 1)
@@ -117,10 +126,17 @@
             copy.start()
 
     send_left((0, 0), "ZA", to_pair, (0, 1))
+
     send_left((0, 0), "XA", to_right, (-1, 0))
     send_left((0, 0), "XB", to_left, (1, 0))
+
     send_left((0, 0), "XB", to_right, (-1, 0))
     send_left((0, 0), "XA", to_left, (1, 0))
+
+    send_left((0, 0), "ZB", to_pair, (0, 1))
+
+    send_left((0, 0), "ZA", to_right, (-1, 0))
+    send_left((0, 0), "ZB", to_left, (1, 0))
 
     @pl.when(home)
     def _():
@@ -140,6 +156,7 @@
         send(picked.at[lax.rem(part + o, 4)], given.at[o - 1], pick_send.at[o - 1], pick_recv.at[o - 1], group[o - 1])
         for o in range(1, 4)
     ]
+
     for copy in pick_copies:
         copy.wait_recv()
     total = picked[part].astype(jnp.float32)
@@ -147,26 +164,25 @@
         total = total + given[o].astype(jnp.float32)
     mixed[...] = total.astype(jnp.bfloat16)
     slab = y * 2 + k
-    offer_copy = send(mixed, right.at[2 * (2 * (1 - zl) + part // 2) + k, lax.rem(x + 2, 4)], offer_send.at[0], offer_recv.at[0], (offer_row, target))
-    meta_copies = [
-        send(meta.at[0], meta.at[o + 1], meta_send.at[o], meta_recv.at[o], mates[o]) for o in range(COLS - 1)
-    ]
-
-    send_left((0, 0), "ZB", to_pair, (0, 1))
-    send_left((0, 0), "ZA", to_right, (-1, 0))
-    send_left((0, 0), "ZB", to_left, (1, 0))
+    offer_copy = send(mixed, right.at[2 * offer_y + k, lax.rem(x + 2, 4)], offer_send.at[0], offer_recv.at[0], (offer_row, target))
+
     send_left((0, 0), "ZB", to_right, (-1, 0))
     send_left((0, 0), "ZA", to_left, (1, 0))
+
     send_left((0, 0), "XA", to_pair, (0, 1))
+
     send_left((0, 0), "XB", to_pair, (0, 1))
 
     arrived((-1, 0), "XA")
     send_left((-1, 0), "XA", to_right, (2, 0))
     arrived((1, 0), "XB")
     send_left((1, 0), "XB", to_left, (2, 0))
+
     arrived((0, 1), "ZA")
     send_left((0, 1), "ZA", to_right, (-1, 1))
-    send_left((0, 1), "ZA", to_left, (1, 1))
+    arrived((0, 1), "ZB")
+    send_left((0, 1), "ZB", to_left, (1, 1))
+
     offer_copy.wait_recv()
 
     def send_right(block, sem, device):
@@ -182,23 +198,32 @@
 
     spread_block(0)
 
+    arrived((-1, 0), "XA")
     send_left((-1, 0), "XA", to_pair, (-1, 1))
+    arrived((1, 0), "XB")
     send_left((1, 0), "XB", to_pair, (1, 1))
+
+    meta_copies = [
+        send(meta.at[0], meta.at[o + 1], meta_send.at[o], meta_recv.at[o], mates[o]) for o in range(COLS - 1)
+    ]
+
     arrived((-1, 0), "XB")
     send_left((-1, 0), "XB", to_pair, (-1, 1))
     arrived((1, 0), "XA")
     send_left((1, 0), "XA", to_pair, (1, 1))
-    arrived((0, 1), "ZB")
-    send_left((0, 1), "ZB", to_left, (1, 1))
-    send_left((0, 1), "ZB", to_right, (-1, 1))
+
     arrived((-1, 0), "ZA")
     send_left((-1, 0), "ZA", to_right, (2, 0))
     arrived((1, 0), "ZB")
     send_left((1, 0), "ZB", to_left, (2, 0))
 
+    send_left((0, 1), "ZB", to_right, (-1, 1))
+    send_left((0, 1), "ZA", to_left, (1, 1))
+
     for step in (1, 3):
         z_copies[step - 1].wait_recv()
         spread_block(step)
+
     z_copies[1].wait_recv()
     spread_block(2)
     core_copies = [send_right(slab, 15, other_core)]
@@ -206,6 +231,7 @@
     arrived((2, 0), "XA", "XB")
     send_left((2, 0), "XA", to_pair, (2, 1))
     send_left((2, 0), "XB", to_pair, (2, 1))
+
     arrived((-1, 1), "ZA")
     send_left((-1, 1), "ZA", to_right, (2, 1))
     arrived((1, 1), "ZB")
@@ -220,6 +246,7 @@
         for step in range(4):
             y_copies[(step, o)].wait_recv()
         core_copies.append(send_right(lax.rem(y + (3 - o), 4) * 2 + k, 16 + o, other_core))
+
     load_table.wait()
     for copy in core_copies:
         copy.wait_recv()
@@ -227,10 +254,10 @@
     def multiply(source, first):
         column = column_of(*source)
         entry = lax.rem(c - column + COLS, COLS)
-        depth, base = lax.rem(column // 2 + 2, 4), 4 * (1 - lax.rem(column, 2))
+        depth = lax.rem(column // 2 + 2, 4)
         factor = jnp.concatenate(
             [
-                jnp.concatenate([right[base + 2 * b + j, depth] for j in range(2)], axis=1)
+                jnp.concatenate([right[2 * held_at(column, b, c) + j, depth] for j in range(2)], axis=1)
                 for b in range(2)
             ],
             axis=0,

time: 50 us -> 47.2 us (0.944)
  Pallas kernels: 47.7 us -> 44.9 us
    pallas_call x1, Pallas kernels: 47.7 us -> 44.9 us  [per_device(): pl.pallas_call(kernel, out_shape=jax.ShapeDtypeStruct((RL, 2, BLK, BLK),...]
where the time goes in v4:
time: 47.2 us; the launch traced here: 47.1 us
  Pallas kernels  44.9 us (95%)
  local copies, waits for them, and re-layouts  1.49 us (3%)
  between operations  0.66 us (1%)
    pallas_call x1, Pallas kernels, per_device(): pl.pallas_call(kernel, out_shape=jax.ShapeDtypeStruct((RL, 2, BLK, BLK),...  44.9 us
    unnamed x1, local copies, waits for them, and re-layouts  1.49 us

profile of v4, /device:TPU:1, one launch (start us, length us, event | category | flops | bytes accessed | tf_op | source)
XLA Modules:
  0.0 47.1 jit_solution(10550784807052300545)
XLA Ops:
  0.7 44.9 %shard_map.55 = f32[20,2,128,128]{3,2,1,0:T(8,128)S(1)} custom-call(bf16[1,1,16,128,128]{4,3,2,1,0:T(8,128)(2,1)} %blocks_ref.1, s32[1,1,16]{2,1,0:T(1,128)} %rows_ref.1, s32[1,1,16]{2,1,0:T(1,128)} %cols_ref.1, s32[1,2]{1,0:T(1,128)} %window_ref.1, s32[1,1]{1,0:T(1,128)S(6)} %copy.7.counts_ref), custom_call_target="tpu_custom_call" | custom-call | flops 2684354560 | bytes 8388608 | tf_op jit(solution)/shard_map/pallas_call | solution.py:309
  45.6 1.5 %copy.8 = f32[20,2,128,128]{3,2,1,0:T(8,128)} copy(f32[20,2,128,128]{3,2,1,0:T(8,128)S(1)} %shard_map.55) | data formatting | bytes 5242880

commit v5 on v4

--- a/solution.py
+++ b/solution.py
@@ -52,19 +52,77 @@
     near = jnp.where(lax.rem(sender_column + c, 2) == 0, 1 - lax.rem(y, 2), lax.rem(y, 2))
     offer_sender = (4 * c + 2 * near + k, sender_column)
 
+    loads = [
+        pltpu.make_async_copy(src, dst, local_sem.at[i])
+        for i, (src, dst) in enumerate(
+            [(rows_ref, rows), (cols_ref, cols), (blocks_ref.at[0, 0], own.at[pl.ds(0, SLOTS)])]
+        )
+    ]
+    for load in loads:
+        load.start()
+
     barrier = pltpu.get_barrier_semaphore()
     senders = mates + z_mates + y_mates + group + [offer_sender] + [other_core]
     for sender in senders:
         pl.semaphore_signal(barrier, inc=1, device_id=sender, device_id_type=MESH)
 
-    loads = [
-        pltpu.make_async_copy(src, dst, local_sem.at[i])
-        for i, (src, dst) in enumerate(
-            [(rows_ref, rows), (cols_ref, cols), (blocks_ref.at[0, 0], own.at[pl.ds(0, SLOTS)])]
-        )
-    ]
-    for load in loads:
-        load.start()
+    pl.semaphore_wait(barrier, len(senders))
+
+    started = []
+
+    def copy_to(src, dst, send_sem, recv_sem, device):
+        return pltpu.make_async_remote_copy(
+            src_ref=src, dst_ref=dst, send_sem=send_sem, recv_sem=recv_sem, device_id=device, device_id_type=MESH
+        )
+
+    def send(*what):
+        copy = copy_to(*what)
+        copy.start()
+        started.append(copy)
+        return copy
+
+    left, seen = {}, set()
+
+    def send_left(source, chunk, column, lands):
+        first, size = CHUNKS[chunk]
+        sem = len(left)
+        left[(lands, chunk)] = send(
+            store[source].at[pl.ds(first, size)], store[lands].at[pl.ds(first, size)],
+            left_send.at[sem], left_recv.at[sem], (r, column),
+        )
+
+    def arrived(lands, *chunks):
+        for chunk in chunks:
+            if (lands, chunk) not in seen:
+                seen.add((lands, chunk))
+                left[(lands, chunk)].wait_recv()
+
+    window_copies = [
+        copy_to(window_ref, window, window_send.at[o], window_recv.at[0], mates[o]) for o in range(COLS - 1)
+    ]
+    home = target == c
+    load_window = pltpu.make_async_copy(window_ref, window, local_sem.at[4])
+
+    @pl.when(home)
+    def _():
+        load_window.start()
+        for copy in window_copies:
+            copy.start()
+
+    loads[2].wait()
+    send_left((0, 0), "ZA", to_pair, (0, 1))
+
+    send_left((0, 0), "XA", to_right, (-1, 0))
+    send_left((0, 0), "XB", to_left, (1, 0))
+
+    send_left((0, 0), "XB", to_right, (-1, 0))
+    send_left((0, 0), "XA", to_left, (1, 0))
+
+    send_left((0, 0), "ZB", to_pair, (0, 1))
+
+    send_left((0, 0), "ZA", to_right, (-1, 0))
+    send_left((0, 0), "ZB", to_left, (1, 0))
+
     for source in SOURCES:
         store[source][NONE] = jnp.zeros((BLK, BLK), jnp.bfloat16)
     for load in loads[:2]:
@@ -80,63 +138,6 @@
     load_own_table = pltpu.make_async_copy(meta.at[0], own_table, local_sem.at[3])
     load_own_table.start()
     load_own_table.wait()
-    loads[2].wait()
-
-    pl.semaphore_wait(barrier, len(senders))
-
-    started = []
-
-    def copy_to(src, dst, send_sem, recv_sem, device):
-        return pltpu.make_async_remote_copy(
-            src_ref=src, dst_ref=dst, send_sem=send_sem, recv_sem=recv_sem, device_id=device, device_id_type=MESH
-        )
-
-    def send(*what):
-        copy = copy_to(*what)
-        copy.start()
-        started.append(copy)
-        return copy
-
-    left, seen = {}, set()
-
-    def send_left(source, chunk, column, lands):
-        first, size = CHUNKS[chunk]
-        sem = len(left)
-        left[(lands, chunk)] = send(
-            store[source].at[pl.ds(first, size)], store[lands].at[pl.ds(first, size)],
-            left_send.at[sem], left_recv.at[sem], (r, column),
-        )
-
-    def arrived(lands, *chunks):
-        for chunk in chunks:
-            if (lands, chunk) not in seen:
-                seen.add((lands, chunk))
-                left[(lands, chunk)].wait_recv()
-
-    window_copies = [
-        copy_to(window_ref, window, window_send.at[o], window_recv.at[0], mates[o]) for o in range(COLS - 1)
-    ]
-    home = target == c
-    load_window = pltpu.make_async_copy(window_ref, window, local_sem.at[4])
-
-    @pl.when(home)
-    def _():
-        load_window.start()
-        for copy in window_copies:
-            copy.start()
-
-    send_left((0, 0), "ZA", to_pair, (0, 1))
-
-    send_left((0, 0), "XA", to_right, (-1, 0))
-    send_left((0, 0), "XB", to_left, (1, 0))
-
-    send_left((0, 0), "XB", to_right, (-1, 0))
-    send_left((0, 0), "XA", to_left, (1, 0))
-
-    send_left((0, 0), "ZB", to_pair, (0, 1))
-
-    send_left((0, 0), "ZA", to_right, (-1, 0))
-    send_left((0, 0), "ZB", to_left, (1, 0))
 
     @pl.when(home)
     def _():
@@ -286,9 +287,11 @@
         (1, 1): ("ZA", "XA", "XB"),
         (2, 1): ("ZA", "ZB", "XA", "XB"),
     }
-    for source in SOURCES:
-        arrived(source, *waits[source])
-        multiply(source, source == (0, 0))
+    for group in (SOURCES[:5], SOURCES[5:]):
+        for source in group:
+            arrived(source, *waits[source])
+        for source in group:
+            multiply(source, source == (0, 0))
 
     for copy in started:
         copy.wait_send()

time: 47.2 us -> 46.9 us (level)
  no operation moved by 1% of the time
where the time goes in v5:
time: 46.9 us; the launch traced here: 46.8 us
  Pallas kernels  44.6 us (95%)
  local copies, waits for them, and re-layouts  1.49 us (3%)
  between operations  0.66 us (1%)
    pallas_call x1, Pallas kernels, per_device(): pl.pallas_call(kernel, out_shape=jax.ShapeDtypeStruct((RL, 2, BLK, BLK),...  44.6 us
    unnamed x1, local copies, waits for them, and re-layouts  1.49 us

profile of v5, /device:TPU:1, one launch (start us, length us, event | category | flops | bytes accessed | tf_op | source)
XLA Modules:
  0.0 46.8 jit_solution(9521584051091659964)
XLA Ops:
  0.7 44.6 %shard_map.55 = f32[20,2,128,128]{3,2,1,0:T(8,128)S(1)} custom-call(bf16[1,1,16,128,128]{4,3,2,1,0:T(8,128)(2,1)} %blocks_ref.1, s32[1,1,16]{2,1,0:T(1,128)} %rows_ref.1, s32[1,1,16]{2,1,0:T(1,128)} %cols_ref.1, s32[1,2]{1,0:T(1,128)} %window_ref.1, s32[1,1]{1,0:T(1,128)S(6)} %copy.7.counts_ref), custom_call_target="tpu_custom_call" | custom-call | flops 2684354560 | bytes 8388608 | tf_op jit(solution)/shard_map/pallas_call | solution.py:312
  45.3 1.5 %copy.8 = f32[20,2,128,128]{3,2,1,0:T(8,128)} copy(f32[20,2,128,128]{3,2,1,0:T(8,128)S(1)} %shard_map.55) | data formatting | bytes 5242880
